TPU v7x, 256 devices: a whole 4x4x8 slice. The times are simulated.
256 devices in a mesh: pts: 16 (over x_hi, z), fn: 16 (over x_lo, y, core).
Axes of the slice: x: 4 (x_hi: 2, x_lo: 2; x = x_hi * 2 + x_lo), y: 4, z: 8, core: 2. Of those that a mesh axis runs over, the one named last changes fastest.
Arguments:
- grad_out: bfloat16 [128, 131072], P('fn', 'pts'), may hold values from -0.0390625 to 0.0390625
- coef: bfloat16 [128, 512], P('fn'), may hold values from -0.5 to 0.5
- coords: float32 [3, 131072], P(None, 'pts'), may hold values from -1 to 1
- w_first: float32 [3, 512], replicated, may hold values from -3.5 to 3.5
- b_first: float32 [512], replicated, may hold values from -3 to 3
- w_second: bfloat16 [512, 512], replicated, may hold values from -0.25 to 0.25
- b_second: float32 [512], replicated, may hold values from -3 to 3
- w_third: bfloat16 [512, 512], replicated, may hold values from -0.25 to 0.25
- b_third: float32 [512], replicated, may hold values from -4 to 4
Outputs:
- grad_coef: float32 [128, 512], P('fn', 'pts')
- grad_w_first: float32 [3, 512], replicated
- grad_b_first: float32 [512], replicated
- grad_w_second: float32 [512, 512], replicated
- grad_b_second: float32 [512], replicated
- grad_w_third: float32 [512, 512], replicated
- grad_b_third: float32 [512], replicated
All inputs are finite; a program needn't handle non-finite values.
Results may differ from a plain program's by a relative error of at most 0.012.
The roundings to bfloat16 on the way count: a program that leaves them out, or rounds other values in their place, can miss the bound.
Values may be sent and summed in bfloat16 or wider, within the bound.
No kernel may reach another device: no remote copies, remote signals or barrier semaphores. Data moves between devices by JAX's collectives and lax.ppermute only.
A program may use at most 128 MiB of HBM per device.

v0:
```python
import jax
import jax.numpy as jnp
from jax import lax
from jax.sharding import PartitionSpec as P


def trunk_forward(points, w_first, b_first, w_second, b_second, w_third, b_third):
    z_one = (
        jnp.dot(
            points.T, w_first, precision=lax.Precision.HIGHEST, preferred_element_type=jnp.float32
        )
        + b_first
    )
    act_one = jnp.tanh(z_one).astype(jnp.bfloat16)
    act_two = jnp.tanh(
        jnp.dot(act_one, w_second, preferred_element_type=jnp.float32) + b_second
    ).astype(jnp.bfloat16)
    basis = (jnp.dot(act_two, w_third, preferred_element_type=jnp.float32) + b_third).astype(
        jnp.bfloat16
    )
    return (act_one, act_two, basis)


def trunk_backward(points, act_one, act_two, grad_basis, w_second, w_third):
    grad_w_third = jnp.dot(act_two.T, grad_basis, preferred_element_type=jnp.float32)
    grad_b_third = jnp.sum(grad_basis.astype(jnp.float32), axis=0)
    two_f = act_two.astype(jnp.float32)
    pre_two = (
        jnp.dot(grad_basis, w_third.T, preferred_element_type=jnp.float32) * (1.0 - two_f * two_f)
    ).astype(jnp.bfloat16)
    grad_w_second = jnp.dot(act_one.T, pre_two, preferred_element_type=jnp.float32)
    grad_b_second = jnp.sum(pre_two.astype(jnp.float32), axis=0)
    one_f = act_one.astype(jnp.float32)
    pre_one = jnp.dot(pre_two, w_second.T, preferred_element_type=jnp.float32) * (
        1.0 - one_f * one_f
    )
    grad_w_first = jnp.dot(
        points, pre_one, precision=lax.Precision.HIGHEST, preferred_element_type=jnp.float32
    )
    grad_b_first = jnp.sum(pre_one, axis=0)
    return (grad_w_first, grad_b_first, grad_w_second, grad_b_second, grad_w_third, grad_b_third)


def shards(grad_out, coef, coords, w_first, b_first, w_second, b_second, w_third, b_third):
    share = grad_out.shape[1] // lax.axis_size("fn")
    offset = lax.axis_index("fn") * share
    own_points = lax.dynamic_slice_in_dim(coords, offset, share, 1)
    act_one, act_two, basis = trunk_forward(
        coords, w_first, b_first, w_second, b_second, w_third, b_third
    )
    partial_value = jnp.dot(grad_out, basis, preferred_element_type=jnp.float32)
    grad_basis = lax.psum_scatter(
        lax.dot_general(
            grad_out, coef, (((0,), (0,)), ((), ())), preferred_element_type=jnp.float32
        ),
        "fn",
        scatter_dimension=0,
        tiled=True,
    ).astype(jnp.bfloat16)
    own_one = lax.dynamic_slice_in_dim(act_one, offset, share, 0)
    own_two = lax.dynamic_slice_in_dim(act_two, offset, share, 0)
    grads = trunk_backward(own_points, own_one, own_two, grad_basis, w_second, w_third)
    grad_coef = lax.psum_scatter(partial_value, "pts", scatter_dimension=1, tiled=True)
    summed = lax.psum((grads[0], grads[1], grads[2], grads[3], grads[4], grads[5]), ("pts", "fn"))
    return (grad_coef, summed[0], summed[1], summed[2], summed[3], summed[4], summed[5])


def solution(mesh):
    return jax.shard_map(
        shards,
        mesh=mesh,
        in_specs=(P("fn", "pts"), P("fn", None), P(None, "pts"), P(), P(), P(), P(), P(), P()),
        out_specs=(P("fn", "pts"), P(), P(), P(), P(), P(), P()),
        check_vma=False,
    )
```

profile of v0, /device:TPU:2, one launch (start us, length us, event | category | flops | bytes accessed | tf_op | source)
XLA Modules:
  0.0 597.5 jit_solution(12960392394778353244)
XLA Ops:
  7.2 0.0 copy-start
  7.2 0.0 reduce-scatter.5.cloned.1.call-start
  7.2 9.1 %fusion.15 = f32[8192,512]{1,0:T(8,128)} fusion(bf16[8,8192]{1,0:T(8,128)(2,1)} %param.9, bf16[8,512]{1,0:T(8,128)(2,1)} %param.10), kind=kOutput, calls=%fused_computation.22 | convolution fusion | flops 67108864 | bytes 16916480 | tf_op jit(solution)/shard_map/dot_general | solution.py:53
  16.3 0.0 reduce-scatter.5.cloned.1.call-update
  16.3 0.0 copy-start.8
  16.3 0.0 reduce-scatter.7.cloned.1.call-start
  16.4 0.8 copy-done.5
  17.2 14.6 %tanh_convert_fusion.1 = bf16[8192,512]{1,0:T(8,128)(2,1)S(1)} fusion(f32[3,8192]{1,0:T(4,128)S(1)} %copy-done.5, f32[3,512]{1,0:T(4,128)S(1)} %copy-done.6, f32[512]{0:T(512)S(1)} %copy-done.7), kind=kOutput, calls=%fused_computation.2 | convolution fusion | flops 159383552 | bytes 8495104 | tf_op jit(solution)/shard_map/dot_general | solution.py:9
  31.8 0.0 copy-start.4
  31.8 3.2 copy-done.4
  35.0 0.0 copy-done
  35.0 0.0 copy-start.9
  35.0 6.7 %tanh_convert_fusion = bf16[8192,512]{1,0:T(8,128)(2,1)} fusion(bf16[8192,512]{1,0:T(8,128)(2,1)S(1)} %tanh_convert_fusion.1, bf16[512,512]{1,0:T(8,128)(2,1)S(1)} %copy-done, f32[512]{0:T(512)S(1)} %copy-done.8), kind=kOutput, calls=%fused_computation.1 | convolution fusion | flops 4303355904 | bytes 17303552 | tf_op jit(solution)/shard_map/dot_general | solution.py:16
  41.7 0.0 copy-done.2
  41.7 8.0 %fusion.2 = f32[8,512]{1,0:T(8,128)S(1)} fusion(bf16[8,8192]{1,0:T(8,128)(2,1)S(1)} %copy-done.3, bf16[8192,512]{1,0:T(8,128)(2,1)} %tanh_convert_fusion, bf16[512,512]{1,0:T(8,128)(2,1)S(1)} %copy-done.2, f32[512]{0:T(512)S(1)} %copy-done.9), kind=kOutput, calls=%fused_computation.7 | convolution fusion | flops 4370464768 | bytes 9062400 | tf_op jit(solution)/shard_map/dot_general | solution.py:51
  49.7 0.9 copy.16
  50.5 0.0 reduce-scatter.7.cloned.1.call-update
  50.6 0.2 all-reduce.4.cloned.1.call-start
  50.8 68.5 %reduce-scatter.5.cloned.1.call-done = f32[512,512]{1,0:T(8,128)} async-done(((f32[8192,512]{1,0:T(8,128)}), f32[512,512]{1,0:T(8,128)}) %reduce-scatter.5.cloned.1.call-update) | async-done | bytes 1048592 | tf_op jit(solution)/shard_map/reduce_scatter | solution.py:52
  119.3 1.9 convert_reduce_fusion.1
  121.3 2.8 fusion.5
  124.1 2.5 fusion.3
  126.6 0.0 all-reduce.4.cloned.1.call-update
  126.6 191.5 %reduce-scatter.7.cloned.1.call-done = f32[32,8]{1,0:T(8,128)} async-done(((f32[512,8]{1,0:T(8,128)}), f32[32,8]{1,0:T(8,128)}) %reduce-scatter.7.cloned.1.call-update) | async-done | bytes 1040
  318.1 1.4 copy.17
  319.5 0.1 convert_reduce_fusion
  319.6 1.5 fusion.14
  321.1 0.6 fusion.7
  321.8 74.4 %all-reduce = (f32[3,512]{1,0:T(4,128)}, f32[512]{0:T(512)}, f32[512]{0:T(512)}, f32[512]{0:T(512)}) all-reduce(f32[3,512]{1,0:T(4,128)S(1)} %fusion.7, f32[512]{0:T(512)S(1)} %get-tuple-element.13, f32[512]{0:T(512)S(1)} %get-tuple-element.15, f32[512]{0:T(512)S(1)} %convert_reduce_fusion), channel_id=1, replica_groups=mesh['pts'=16,'fn'=16] {'pts','fn'}, use_global_device_ids=true, to_apply=%region_2.0 | all-reduce | flops 3072 | bytes 24576 | tf_op jit(solution)/shard_map/psum | solution.py:64
  396.2 190.3 %all-reduce.4.cloned.1.call-done = (f32[512,512]{1,0:T(8,128)}, f32[512,512]{1,0:T(8,128)}) async-done(((f32[512,512]{1,0:T(8,128)}, f32[512,512]{1,0:T(8,128)}), (f32[512,512]{1,0:T(8,128)}, f32[512,512]{1,0:T(8,128)})) %all-reduce.4.cloned.1.call-update) | async-done | bytes 2097168 | tf_op jit(solution)/shard_map/psum | solution.py:64
  586.5 2.3 copy.20
  588.7 2.3 copy.21
  (12 shorter events, 0.0 us)
Async XLA Ops:
  7.2 27.8 %copy-start = (bf16[512,512]{1,0:T(8,128)(2,1)S(1)}, bf16[512,512]{1,0:T(8,128)(2,1)}, u32[]{:S(2)}) copy-start(bf16[512,512]{1,0:T(8,128)(2,1)} %param.14) | copy-start | bytes 1572868
  7.2 112.2 %reduce-scatter.5.cloned.1.call-start = ((), (), s32[]{:S(2)}) async-start(), calls=%async_computation.2 | async-start | bytes 17825792 | tf_op jit(solution)/shard_map/reduce_scatter | solution.py:52
  16.3 0.9 copy-start.5
  16.3 0.9 copy-start.6
  16.3 0.9 copy-start.7
  16.3 18.7 %copy-start.8 = (f32[512]{0:T(512)S(1)}, f32[512]{0:T(512)}, u32[]{:S(2)}) copy-start(f32[512]{0:T(512)} %param.15) | copy-start | bytes 6148
  16.3 301.8 %reduce-scatter.7.cloned.1.call-start = ((), (), s32[]{:S(2)}) async-start(), calls=%async_computation.3 | async-start | bytes 278528
  31.8 3.2 copy-start.4
  35.0 6.7 %copy-start.2 = (bf16[512,512]{1,0:T(8,128)(2,1)S(1)}, bf16[512,512]{1,0:T(8,128)(2,1)}, u32[]{:S(2)}) copy-start(bf16[512,512]{1,0:T(8,128)(2,1)} %param.16) | copy-start | bytes 1572868
  35.0 6.7 %copy-start.3 = (bf16[8,8192]{1,0:T(8,128)(2,1)S(1)}, bf16[8,8192]{1,0:T(8,128)(2,1)}, u32[]{:S(2)}) copy-start(bf16[8,8192]{1,0:T(8,128)(2,1)} %param.9) | copy-start | bytes 393220
  35.0 6.7 %copy-start.9 = (f32[512]{0:T(512)S(1)}, f32[512]{0:T(512)}, u32[]{:S(2)}) copy-start(f32[512]{0:T(512)} %param.17) | copy-start | bytes 6148
  50.6 535.9 %all-reduce.4.cloned.1.call-start = ((), (), s32[]{:S(2)}) async-start(), calls=%async_computation.4 | async-start | bytes 4194304 | tf_op jit(solution)/shard_map/psum | solution.py:64
  119.3 200.2 %copy-start.1 = (f32[512,512]{1,0:T(8,128)S(1)}, f32[512,512]{1,0:T(8,128)}, u32[]{:S(2)}) copy-start(f32[512,512]{1,0:T(8,128)} %reduce-scatter.5.cloned.1.call-done) | copy-start | bytes 3145732
Sparse Core Ops, SparseCore 0:
  16.4 102.8 reduce-scatter.4
  123.1 194.9 reduce-scatter.6
  325.2 261.2 all-reduce.3
where the time goes:
time: 598 us
  waiting for transfers between devices  450 us (75%)
  blocking collectives  74.4 us (12%)
  matrix products  47.7 us (8%)
  between operations  13.8 us (2%)
  local copies, waits for them, and re-layouts  10.8 us (2%)
    unnamed x4, waiting for transfers between devices  192 us
    psum x1, waiting for transfers between devices, shards(): lax.psum((grads[0], grads[1], grads[2], grads[3], grads[4], grads[5]), ('...  190 us
    psum x1, blocking collectives, shards(): lax.psum((grads[0], grads[1], grads[2], grads[3], grads[4], grads[5]), ('...  74.4 us
    reduce_scatter x1, waiting for transfers between devices, shards(): lax.psum_scatter(lax.dot_general(grad_out, coef, (((0,), (0,)), ((), ()))...  68.5 us
    dot_general x1, matrix products, trunk_forward(): jnp.dot(points.T, w_first, precision=lax.Precision.HIGHEST, preferred_ele...  14.6 us
  transfers between devices with their start and end apart: 3, of which 3 were waited for; matrix products, arithmetic and copies ran while one was open for 7% of the time, Pallas kernels for 0%

commit v1 on v0

--- a/solution.py
+++ b/solution.py
@@ -61,7 +61,9 @@
     own_two = lax.dynamic_slice_in_dim(act_two, offset, share, 0)
     grads = trunk_backward(own_points, own_one, own_two, grad_basis, w_second, w_third)
     grad_coef = lax.psum_scatter(partial_value, "pts", scatter_dimension=1, tiled=True)
-    summed = lax.psum((grads[0], grads[1], grads[2], grads[3], grads[4], grads[5]), ("pts", "fn"))
+    summed = lax.psum(
+        lax.psum((grads[0], grads[1], grads[2], grads[3], grads[4], grads[5]), "pts"), "fn"
+    )
     return (grad_coef, summed[0], summed[1], summed[2], summed[3], summed[4], summed[5])
 
 

time: 598 us -> 630 us (1.054)
  blocking collectives: 74.4 us -> 128 us
  waiting for transfers between devices: 450 us -> 428 us
    psum x1 -> x2, blocking collectives: 74.4 us -> 128 us  [the longest x1 74.6 us: shards(): lax.psum((grads[0], grads[1], grads[2], grads[3], grads[4], grads[5]), 'p...]
    psum x1 -> x2, waiting for transfers between devices: 190 us -> 153 us  [the longest x1 153 us: shards(): lax.psum((grads[0], grads[1], grads[2], grads[3], grads[4], grads[5]), 'p...]
    reduce_scatter x1, waiting for transfers between devices: 68.5 us -> 77.7 us  [shards(): lax.psum_scatter(lax.dot_general(grad_out, coef, (((0,), (0,)), ((), ()))...]
    unnamed x4 -> x5, waiting for transfers between devices: 192 us -> 198 us
  transfers between devices with their start and end apart: 3 -> 4, of which waited for: 3 -> 3; matrix products, arithmetic and copies ran while one was open for 7% -> 5% of each run, Pallas kernels for 0% -> 0%
where the time goes in v1:
time: 630 us; the launch traced here: 629 us
  waiting for transfers between devices  428 us (68%)
  blocking collectives  128 us (20%)
  matrix products  47.6 us (8%)
  between operations  13.8 us (2%)
  local copies, waits for them, and re-layouts  10.8 us (2%)
    unnamed x5, waiting for transfers between devices  198 us
    psum x1, waiting for transfers between devices, shards(): lax.psum((grads[0], grads[1], grads[2], grads[3], grads[4], grads[5]), 'p...  153 us
    reduce_scatter x1, waiting for transfers between devices, shards(): lax.psum_scatter(lax.dot_general(grad_out, coef, (((0,), (0,)), ((), ()))...  77.7 us
    psum x1, blocking collectives, shards(): lax.psum((grads[0], grads[1], grads[2], grads[3], grads[4], grads[5]), 'p...  74.6 us
    psum x1, blocking collectives, shards(): lax.psum(lax.psum((grads[0], grads[1], grads[2], grads[3], grads[4], grad...  53.6 us
    dot_general x1, matrix products, trunk_forward(): jnp.dot(points.T, w_first, precision=lax.Precision.HIGHEST, preferred_ele...  14.6 us
  transfers between devices with their start and end apart: 4, of which 3 were waited for; matrix products, arithmetic and copies ran while one was open for 5% of the time, Pallas kernels for 0%

profile of v1, /device:TPU:2, one launch (start us, length us, event | category | flops | bytes accessed | tf_op | source)
XLA Modules:
  0.0 629.1 jit_solution(17606985603073641787)
XLA Ops:
  7.2 0.0 copy-start
  7.2 0.0 reduce-scatter.5.cloned.1.call-start
  7.2 9.1 %fusion.15 = f32[8192,512]{1,0:T(8,128)} fusion(bf16[8,8192]{1,0:T(8,128)(2,1)} %param.9, bf16[8,512]{1,0:T(8,128)(2,1)} %param.10), kind=kOutput, calls=%fused_computation.22 | convolution fusion | flops 67108864 | bytes 16916480 | tf_op jit(solution)/shard_map/dot_general | solution.py:53
  16.3 0.0 reduce-scatter.5.cloned.1.call-update
  16.3 0.0 copy-start.8
  16.3 0.0 all-reduce.9.cloned.1.call-start
  16.4 0.8 copy-done.5
  17.2 0.0 copy-done.6
  17.2 14.6 %tanh_convert_fusion.1 = bf16[8192,512]{1,0:T(8,128)(2,1)S(1)} fusion(f32[3,8192]{1,0:T(4,128)S(1)} %copy-done.5, f32[3,512]{1,0:T(4,128)S(1)} %copy-done.6, f32[512]{0:T(512)S(1)} %copy-done.7), kind=kOutput, calls=%fused_computation.2 | convolution fusion | flops 159383552 | bytes 8495104 | tf_op jit(solution)/shard_map/dot_general | solution.py:9
  31.8 3.2 copy-done.4
  35.0 6.6 %tanh_convert_fusion = bf16[8192,512]{1,0:T(8,128)(2,1)} fusion(bf16[8192,512]{1,0:T(8,128)(2,1)S(1)} %tanh_convert_fusion.1, bf16[512,512]{1,0:T(8,128)(2,1)S(1)} %copy-done, f32[512]{0:T(512)S(1)} %copy-done.8), kind=kOutput, calls=%fused_computation.1 | convolution fusion | flops 4303355904 | bytes 17303552 | tf_op jit(solution)/shard_map/dot_general | solution.py:16
  41.7 77.7 %reduce-scatter.5.cloned.1.call-done = f32[512,512]{1,0:T(8,128)} async-done(((f32[8192,512]{1,0:T(8,128)}), f32[512,512]{1,0:T(8,128)}) %reduce-scatter.5.cloned.1.call-update) | async-done | bytes 1048592 | tf_op jit(solution)/shard_map/reduce_scatter | solution.py:52
  119.3 1.9 convert_reduce_fusion.1
  121.2 2.5 fusion.3
  123.7 2.8 fusion.5
  126.5 0.0 all-reduce.9.cloned.1.call-update
  126.6 0.0 reduce-scatter.7.cloned.1.call-start
  126.6 8.0 %fusion.2 = f32[8,512]{1,0:T(8,128)S(1)} fusion(bf16[8,8192]{1,0:T(8,128)(2,1)S(1)} %copy-done.3, bf16[8192,512]{1,0:T(8,128)(2,1)} %tanh_convert_fusion, bf16[512,512]{1,0:T(8,128)(2,1)S(1)} %copy-done.2, f32[512]{0:T(512)S(1)} %copy-done.9), kind=kOutput, calls=%fused_computation.7 | convolution fusion | flops 4370464768 | bytes 9062400 | tf_op jit(solution)/shard_map/dot_general | solution.py:51
  134.6 0.9 copy.16
  135.5 0.0 reduce-scatter.7.cloned.1.call-update
  135.5 0.0 all-reduce.7.cloned.1.call-start
  135.5 153.2 %all-reduce.9.cloned.1.call-done = (f32[512,512]{1,0:T(8,128)}, f32[512,512]{1,0:T(8,128)}) async-done(((f32[512,512]{1,0:T(8,128)}, f32[512,512]{1,0:T(8,128)}), (f32[512,512]{1,0:T(8,128)}, f32[512,512]{1,0:T(8,128)})) %all-reduce.9.cloned.1.call-update) | async-done | bytes 2097168 | tf_op jit(solution)/shard_map/psum | solution.py:65
  288.8 0.0 all-reduce.7.cloned.1.call-update
  288.8 197.5 %reduce-scatter.7.cloned.1.call-done = f32[32,8]{1,0:T(8,128)} async-done(((f32[512,8]{1,0:T(8,128)}), f32[32,8]{1,0:T(8,128)}) %reduce-scatter.7.cloned.1.call-update) | async-done | bytes 1040
  486.3 1.4 copy.17
  487.7 0.1 convert_reduce_fusion
  487.8 1.5 fusion.14
  489.3 0.6 fusion.7
  489.9 74.6 %all-reduce.2 = (f32[3,512]{1,0:T(4,128)S(1)}, f32[512]{0:T(512)S(1)}, f32[512]{0:T(512)S(1)}, f32[512]{0:T(512)S(1)}) all-reduce(f32[3,512]{1,0:T(4,128)S(1)} %fusion.7, f32[512]{0:T(512)S(1)} %get-tuple-element.19, f32[512]{0:T(512)S(1)} %get-tuple-element.21, f32[512]{0:T(512)S(1)} %convert_reduce_fusion), channel_id=1, replica_groups=mesh['pts'=16,'fn'=16] {'pts'}, use_global_device_ids=true, to_apply=%region_2.0 | all-reduce | flops 3072 | bytes 24576 | tf_op jit(solution)/shard_map/psum | solution.py:65
  564.5 53.6 %all-reduce = (f32[3,512]{1,0:T(4,128)}, f32[512]{0:T(512)}, f32[512]{0:T(512)}, f32[512]{0:T(512)}) all-reduce(f32[3,512]{1,0:T(4,128)S(1)} %get-tuple-element.13, f32[512]{0:T(512)S(1)} %get-tuple-element.14, f32[512]{0:T(512)S(1)} %get-tuple-element.15, f32[512]{0:T(512)S(1)} %get-tuple-element.16), channel_id=1, replica_groups=mesh['pts'=16,'fn'=16] {'fn'}, use_global_device_ids=true, to_apply=%region_3.0 | all-reduce | flops 3072 | bytes 24576 | tf_op jit(solution)/shard_map/psum | solution.py:64
  618.1 2.3 copy.22
  620.3 2.3 copy.23
  (16 shorter events, 0.0 us)
Async XLA Ops:
  7.2 27.9 %copy-start = (bf16[512,512]{1,0:T(8,128)(2,1)S(1)}, bf16[512,512]{1,0:T(8,128)(2,1)}, u32[]{:S(2)}) copy-start(bf16[512,512]{1,0:T(8,128)(2,1)} %param.14) | copy-start | bytes 1572868
  7.2 112.2 %reduce-scatter.5.cloned.1.call-start = ((), (), s32[]{:S(2)}) async-start(), calls=%async_computation.2 | async-start | bytes 17825792 | tf_op jit(solution)/shard_map/reduce_scatter | solution.py:52
  16.3 0.9 copy-start.5
  16.3 0.9 copy-start.6
  16.3 0.9 copy-start.7
  16.3 18.7 %copy-start.8 = (f32[512]{0:T(512)S(1)}, f32[512]{0:T(512)}, u32[]{:S(2)}) copy-start(f32[512]{0:T(512)} %param.15) | copy-start | bytes 6148
  16.3 272.4 %all-reduce.9.cloned.1.call-start = ((), (), s32[]{:S(2)}) async-start(), calls=%async_computation.5 | async-start | bytes 4194304 | tf_op jit(solution)/shard_map/psum | solution.py:65
  31.8 3.2 copy-start.4
  35.0 84.3 %copy-start.2 = (bf16[512,512]{1,0:T(8,128)(2,1)S(1)}, bf16[512,512]{1,0:T(8,128)(2,1)}, u32[]{:S(2)}) copy-start(bf16[512,512]{1,0:T(8,128)(2,1)} %param.16) | copy-start | bytes 1572868
  41.7 84.9 %copy-start.3 = (bf16[8,8192]{1,0:T(8,128)(2,1)S(1)}, bf16[8,8192]{1,0:T(8,128)(2,1)}, u32[]{:S(2)}) copy-start(bf16[8,8192]{1,0:T(8,128)(2,1)} %param.9) | copy-start | bytes 393220
  41.7 84.9 %copy-start.9 = (f32[512]{0:T(512)S(1)}, f32[512]{0:T(512)}, u32[]{:S(2)}) copy-start(f32[512]{0:T(512)} %param.17) | copy-start | bytes 6148
  126.5 361.1 %copy-start.1 = (f32[512,512]{1,0:T(8,128)S(1)}, f32[512,512]{1,0:T(8,128)}, u32[]{:S(2)}) copy-start(f32[512,512]{1,0:T(8,128)} %reduce-scatter.5.cloned.1.call-done) | copy-start | bytes 3145732
  126.6 359.7 %reduce-scatter.7.cloned.1.call-start = ((), (), s32[]{:S(2)}) async-start(), calls=%async_computation.3 | async-start | bytes 278528
  135.5 482.6 %all-reduce.7.cloned.1.call-start = ((), (), s32[]{:S(2)}) async-start(), calls=%async_computation.4 | async-start | bytes 4194304 | tf_op jit(solution)/shard_map/psum | solution.py:64
Sparse Core Ops, SparseCore 0:
  16.4 102.8 reduce-scatter.4
  126.7 162.0 all-reduce.8
  292.6 193.6 reduce-scatter.6
  489.0 126.5 all-reduce.6
